TPU v7x, 128 devices: a whole 4x4x4 slice. The times are simulated.
128 devices in a mesh: lat: 8 (over y_lo, z), lon: 16 (over x, y_hi, core).
Axes of the slice: x: 4, y: 4 (y_hi: 2, y_lo: 2; y = y_hi * 2 + y_lo), z: 4, core: 2. Of those that a mesh axis runs over, the one named last changes fastest.
Arguments:
- x_first: bfloat16 [192, 768, 512], P('lat', 'lon'), may hold values from -6 to 6
- x_second: bfloat16 [192, 768, 512], P('lat', 'lon'), may hold values from -6 to 6
- cotangent: bfloat16 [192, 768, 512], P('lat', 'lon'), may hold values from -6 to 6
- gain_attn: float32 [512], replicated, may hold values from 0.1 to 1.9
- gain_mlp: float32 [512], replicated, may hold values from 0.1 to 1.9
- w_qkv: bfloat16 [512, 1536], replicated, may hold values from -0.25 to 0.25
- w_out: bfloat16 [512, 512], replicated, may hold values from -0.25 to 0.25
- w_up: bfloat16 [512, 2048], replicated, may hold values from -0.25 to 0.25
- w_down: bfloat16 [2048, 512], replicated, may hold values from -0.125 to 0.125
- bias: float32 [8, 72, 72], replicated, may hold values from -2 to 300, as said below
Outputs:
- out_first: bfloat16 [192, 768, 512], P('lat', 'lon')
- grad_input: bfloat16 [192, 768, 512], P('lat', 'lon')
- grad_up: float32 [512, 2048], P(('lat', 'lon'))
- grad_down: float32 [2048, 512], P(('lat', 'lon'))
Inputs may be any that keep to these rules, and one draw needn't show every extreme that they name: Relative position bias of each head within one window.
All inputs are finite; a program needn't handle non-finite values.
Results may differ from a plain program's by a relative error of at most 0.0065.
Values may be sent and summed in bfloat16 or wider, within the bound.
A program may use at most 128 MiB of HBM per device.

v0:
```python
import jax
import jax.numpy as jnp
from jax import lax
from jax.sharding import PartitionSpec as P

WH = 6
WW = 12


norm_eps = 1e-05


def extended(block, sides, width):
    for axis, dim in sides:
        count = lax.axis_size(axis)
        forward = [(i, i + 1) for i in range(count - 1)]
        forward.append((count - 1, 0))
        backward = [(target, source) for source, target in forward]
        low = lax.ppermute(
            lax.slice_in_dim(block, block.shape[dim] - width, None, axis=dim), axis, forward
        )
        high = lax.ppermute(lax.slice_in_dim(block, 0, width, axis=dim), axis, backward)
        block = jnp.concatenate([low, block, high], axis=dim)
    return block


def normalize(values):
    widened = values.astype(jnp.float32)
    centred = widened - jnp.mean(widened, axis=-1, keepdims=True)
    scale_inv = lax.rsqrt(jnp.mean(centred * centred, axis=-1, keepdims=True) + norm_eps)
    return (centred * scale_inv, scale_inv)


def gelu_value(before):
    return 0.5 * before * (1.0 + jax.scipy.special.erf(before * 0.7071067811865476))


def gelu_slope(before):
    return (
        0.5 * (1.0 + jax.scipy.special.erf(before * 0.7071067811865476))
        + before * jnp.exp(-0.5 * before * before) * 0.3989422804014327
    )


def widen_field(field, shift_h, shift_w):
    padded = extended(field, (("lat", 0), ("lon", 1)), shift_w)
    excess = shift_w - shift_h
    return padded[excess : padded.shape[0] - excess]


def attend(windows, present, bias):
    window_count, window_size, triple = windows.shape
    head_count = bias.shape[0]
    features = triple // 3
    head_size = features // head_count
    pieces = windows.reshape(window_count, window_size, 3, head_count, head_size)
    scores = (
        jnp.einsum(
            "wqhd,wkhd->whqk", pieces[:, :, 0], pieces[:, :, 1], preferred_element_type=jnp.float32
        )
        * head_size ** (-0.5)
        + bias[None]
    )
    scores = jnp.where(present[:, None, None, :], scores, -jnp.inf)
    highest = jnp.max(scores, axis=-1, keepdims=True)
    raised = jnp.exp(scores - highest)
    attention = (raised / jnp.sum(raised, axis=-1, keepdims=True)).astype(jnp.bfloat16)
    blended = jnp.einsum(
        "whqk,wkhd->wqhd", attention, pieces[:, :, 2], preferred_element_type=jnp.float32
    )
    return blended.reshape(window_count, window_size, features).astype(jnp.bfloat16)


def shards(x_first, x_second, cotangent, gain_attn, gain_mlp, w_qkv, w_out, w_up, w_down, bias):
    rows_lat, cols_lon, features = x_first.shape
    shift_h = WH // 2
    shift_w = WW // 2
    centred, scale_inv = normalize(x_first)
    normed = (centred * gain_attn).astype(jnp.bfloat16)
    projected = jnp.dot(
        widen_field(normed, shift_h, shift_w), w_qkv, preferred_element_type=jnp.float32
    ).astype(jnp.bfloat16)
    band_count = rows_lat // WH + 1
    per_band = cols_lon // WW + 1
    triple = projected.shape[2]
    windows = (
        projected.reshape(band_count, WH, per_band, WW, triple)
        .transpose(0, 2, 1, 3, 4)
        .reshape(band_count * per_band, WH * WW, triple)
    )
    lat_index = (
        lax.axis_index("lat") * rows_lat - shift_h + jnp.arange(band_count * WH, dtype=jnp.int32)
    )
    inside = ((lat_index >= 0) & (lat_index < rows_lat * lax.axis_size("lat"))).reshape(
        band_count, WH
    )
    present = jnp.broadcast_to(inside[:, None, :, None], (band_count, per_band, WH, WW)).reshape(
        band_count * per_band, WH * WW
    )
    blended = attend(windows, present, bias)
    attended = (
        blended.reshape(band_count, per_band, WH, WW, features)
        .transpose(0, 2, 1, 3, 4)
        .reshape(band_count * WH, per_band * WW, features)
    )
    attended = attended[shift_h : shift_h + rows_lat, shift_w : shift_w + cols_lon]
    residual = x_first.astype(jnp.float32) + jnp.dot(
        attended, w_out, preferred_element_type=jnp.float32
    )
    mid_centred, mid_scale = normalize(residual)
    normed_mid = (mid_centred * gain_mlp).astype(jnp.bfloat16)
    hidden_first = gelu_value(jnp.dot(normed_mid, w_up, preferred_element_type=jnp.float32)).astype(
        jnp.bfloat16
    )
    out_first = (
        residual + jnp.dot(hidden_first, w_down, preferred_element_type=jnp.float32)
    ).astype(jnp.bfloat16)
    tokens = rows_lat * cols_lon
    flat_x = x_second.reshape(tokens, features)
    flat_cot = cotangent.reshape(tokens, features)
    sec_centred, sec_scale = normalize(flat_x)
    normed_second = (sec_centred * gain_mlp).astype(jnp.bfloat16)
    before = jnp.dot(normed_second, w_up, preferred_element_type=jnp.float32)
    hidden_second = gelu_value(before).astype(jnp.bfloat16)
    contract_last = (((1,), (1,)), ((), ()))
    back_hidden = lax.dot_general(
        flat_cot, w_down, contract_last, preferred_element_type=jnp.float32
    )
    back_before = (back_hidden * gelu_slope(before)).astype(jnp.bfloat16)
    devices = lax.axis_size("lat") * lax.axis_size("lon")
    contract_rows = (((0,), (0,)), ((), ()))
    full_down = lax.dot_general(
        hidden_second, flat_cot, contract_rows, preferred_element_type=jnp.float32
    )
    full_up = lax.dot_general(
        normed_second, back_before, contract_rows, preferred_element_type=jnp.float32
    )
    summed_down, summed_up = (
        lax.psum_scatter(full_down, ("lat", "lon"), scatter_dimension=0, tiled=True),
        lax.psum_scatter(full_up, ("lat", "lon"), scatter_dimension=0, tiled=True),
    )
    back_norm = (
        lax.dot_general(back_before, w_up, contract_last, preferred_element_type=jnp.float32)
        * gain_mlp
    )
    grad_rows = flat_cot.astype(jnp.float32) + sec_scale * (
        back_norm
        - jnp.mean(back_norm, axis=-1, keepdims=True)
        - sec_centred * jnp.mean(back_norm * sec_centred, axis=-1, keepdims=True)
    )
    grad_input = grad_rows.astype(jnp.bfloat16).reshape(rows_lat, cols_lon, features)
    return (out_first, grad_input, summed_up / devices, summed_down / devices)


def solution(mesh):
    in_specs = (
        P("lat", "lon", None),
        P("lat", "lon", None),
        P("lat", "lon", None),
        P(),
        P(),
        P(),
        P(),
        P(),
        P(),
        P(),
    )
    out_specs = (
        P("lat", "lon", None),
        P("lat", "lon", None),
        P(("lat", "lon"), None),
        P(("lat", "lon"), None),
    )
    return jax.shard_map(shards, mesh=mesh, in_specs=in_specs, out_specs=out_specs, check_vma=False)
```

profile of v0, /device:TPU:1, one launch (start us, length us, event | category | flops | bytes accessed | tf_op | source)
XLA Modules:
  0.0 836.2 jit_solution(7226646217407187591)
XLA Ops:
  11.3 2.6 fusion.71
  14.0 5.4 fusion.5
  19.4 2.2 copy-done.4
  21.7 4.5 fusion.72
  26.3 7.3 fusion.7
  35.2 1.9 fusion.21
  37.7 2.5 collective-permute-start
  40.2 3.5 collective-permute-start.1
  43.7 3.0 fusion.66
  46.7 5.4 collective-permute-done
  53.2 3.9 collective-permute-start.2
  60.2 5.8 collective-permute-done.2
  66.0 3.1 collective-permute-done.3
  69.1 7.9 convolution_convert_fusion
  77.0 8.8 %reshape.109 = bf16[5,6,5,12,1536]{4,3,2,1,0:T(8,128)(2,1)} reshape(bf16[30,60,1536]{2,1,0:T(8,128)(2,1)} %convolution_convert_fusion) | data formatting | bytes 11059200 | tf_op jit(solution)/shard_map/reshape | solution.py:87
  85.8 7.0 copy.38
  92.8 15.9 %reshape_reshape.3 = bf16[25,72,3,8,64]{4,3,2,1,0:T(8,128)(2,1)} reshape(bf16[5,5,6,12,1536]{4,3,2,1,0:T(8,128)(2,1)} %bitcast.63) | data formatting | bytes 11059200 | tf_op jit(solution)/shard_map/reshape;reshape | solution.py:56
  108.7 7.7 fusion.67
  116.4 6.0 copy.35
  122.4 6.0 copy.36
  128.3 6.0 copy.34
  134.3 5.2 fusion.15
  139.5 3.3 fusion.69
  142.7 2.9 convert_bitcast_fusion
  145.6 6.0 copy.31
  151.7 6.2 convert_element_type.63
  157.9 3.5 copy.32
  161.3 4.0 reshape.110
  165.4 2.4 fusion.70
  169.7 8.6 %add_convert_fusion.1 = bf16[24,48,512]{2,1,0:T(8,128)(2,1)} fusion(f32[24,48,512]{2,1,0:T(8,128)} %copy-done.8, bf16[2048,512]{1,0:T(8,128)(2,1)} %param.18, bf16[512,2048]{1,0:T(8,128)(2,1)S(1)} %copy-done, f32[512]{0:T(512)S(1)} %copy-done.14, f32[24,48]{1,0:T(8,128)S(1)} %add_rsqrt_fusion.1, f32[24,48]{1,0:T(8,128)S(1)} %broadcast_multiply_fusion.2), kind=kOutput, calls=%fused_computation.54 | convolution fusion | flops 4847173632 | bytes 7744512 | tf_op jit(solution)/shard_map/dot_general | solution.py:116
  178.3 11.2 %all-reduce.3.cloned.1.call-done = f32[512,2048]{1,0:T(8,128)} async-done(((f32[512,2048]{1,0:T(8,128)}), f32[512,2048]{1,0:T(8,128)}) %all-reduce.3.cloned.1.call-update) | async-done | bytes 4194320
  191.0 637.0 %reduce-scatter.2.cloned.1.call-done = f32[16,512]{1,0:T(8,128)} async-done(((f32[2048,512]{1,0:T(8,128)}), f32[16,512]{1,0:T(8,128)}) %reduce-scatter.2.cloned.1.call-update) | async-done | bytes 32784 | tf_op jit(solution)/shard_map/reduce_scatter | solution.py:139
  (63 shorter events, 15.2 us)
Async XLA Ops:
  7.2 4.1 copy-start
  7.2 3.7 copy-start.1
  7.2 3.7 copy-start.14
  7.2 182.3 %all-reduce.3.cloned.1.call-start = ((), (), s32[]{:S(2)}) async-start(), calls=%async_computation.2 | async-start | bytes 8388608
  11.3 2.7 copy-start.9
  11.3 2.7 copy-start.15
  14.0 5.5 copy-start.16
  19.4 2.2 copy-start.4
  26.2 801.8 %reduce-scatter.2.cloned.1.call-start = ((), (), s32[]{:S(2)}) async-start(), calls=%async_computation.1 | async-start | bytes 4227072 | tf_op jit(solution)/shard_map/reduce_scatter | solution.py:139
  33.5 3.6 copy-start.13
  33.6 3.6 copy-start.2
  35.2 8.5 %copy-start.5 = (bf16[1152,2048]{1,0:T(8,128)(2,1)S(1)}, bf16[1152,2048]{1,0:T(8,128)(2,1)}, u32[]{:S(2)}) copy-start(bf16[1152,2048]{1,0:T(8,128)(2,1)} %copy-done.4) | copy-start | bytes 14155780
  37.6 14.6 %copy-start.6 = (bf16[24,48,512]{2,1,0:T(8,128)(2,1)}, bf16[24,48,512]{2,1,0:T(8,128)(2,1)S(1)}, u32[]{:S(2)}) copy-start(bf16[24,48,512]{2,1,0:T(8,128)(2,1)S(1)} %fusion.23) | copy-start | bytes 3538948
  37.7 14.5 %collective-permute-start = (bf16[6,48,512]{2,1,0:T(8,128)(2,1)S(1)}, bf16[6,48,512]{2,1,0:T(8,128)(2,1)S(1)}, u32[]{:S(2)}, u32[]{:S(2)}) collective-permute-start(bf16[6,48,512]{2,1,0:T(8,128)(2,1)S(1)} %get-tuple-element.11), channel_id=1, source_target_pairs={{0,16},{16,32},{32,48},{48,64},{64,80},{80,96},{96,112},{112,0},{1... | collective-permute-start | bytes 884744 | tf_op jit(solution)/shard_map/ppermute | solution.py:19
  40.2 12.0 %collective-permute-start.1 = (bf16[6,48,512]{2,1,0:T(8,128)(2,1)S(1)}, bf16[6,48,512]{2,1,0:T(8,128)(2,1)S(1)}, u32[]{:S(2)}, u32[]{:S(2)}) collective-permute-start(bf16[6,48,512]{2,1,0:T(8,128)(2,1)S(1)} %get-tuple-element.12), channel_id=1, source_target_pairs={{16,0},{32,16},{48,32},{64,48},{80,64},{96,80},{112,96},{0,112},{1... | collective-permute-start | bytes 884744 | tf_op jit(solution)/shard_map/ppermute | solution.py:22
  46.7 10.3 %copy-start.10 = (bf16[24,48,512]{2,1,0:T(8,128)(2,1)S(1)}, bf16[24,48,512]{2,1,0:T(8,128)(2,1)}, u32[]{:S(2)}) copy-start(bf16[24,48,512]{2,1,0:T(8,128)(2,1)} %param.12) | copy-start | bytes 3538948
  52.1 6.7 copy-start.11
  52.2 6.7 copy-start.12
  53.2 12.8 %collective-permute-start.2 = (bf16[36,6,512]{2,1,0:T(8,128)(2,1)}, bf16[36,6,512]{2,1,0:T(8,128)(2,1)}, u32[]{:S(2)}, u32[]{:S(2)}) collective-permute-start(bf16[36,6,512]{2,1,0:T(8,128)(2,1)} %get-tuple-element.9), channel_id=1, source_target_pairs={{0,1},{1,2},{2,3},{3,4},{4,5},{5,6},{6,7},{7,8},{8,9},{9,10},{10,1... | collective-permute-start | bytes 663560 | tf_op jit(solution)/shard_map/ppermute | solution.py:19
  57.0 12.1 %collective-permute-start.3 = (bf16[36,6,512]{2,1,0:T(8,128)(2,1)}, bf16[36,6,512]{2,1,0:T(8,128)(2,1)}, u32[]{:S(2)}, u32[]{:S(2)}) collective-permute-start(bf16[36,6,512]{2,1,0:T(8,128)(2,1)} %get-tuple-element.10), channel_id=1, source_target_pairs={{1,0},{2,1},{3,2},{4,3},{5,4},{6,5},{7,6},{8,7},{9,8},{10,9},{11,1... | collective-permute-start | bytes 663560 | tf_op jit(solution)/shard_map/ppermute | solution.py:22
  139.5 3.3 copy-start.7
  161.3 4.0 copy-start.3
  167.8 1.4 copy-start.8
Sparse Core Ops, SparseCore 0:
  26.3 163.1 all-reduce.2
  191.9 636.0 reduce-scatter.1
where the time goes:
time: 844 us; the launch traced here: 836 us
  waiting for transfers between devices  663 us (79%)
  local copies, waits for them, and re-layouts  82.2 us (10%)
  matrix products  49.8 us (6%)
  other arithmetic  17.3 us (2%)
  between operations  14.4 us (2%)
  starting transfers between devices  9.99 us (1%)
    reduce_scatter x1, waiting for transfers between devices, shards(): lax.psum_scatter(full_down, ('lat', 'lon'), scatter_dimension=0, tiled=True)  637 us
    unnamed x38, local copies, waits for them, and re-layouts  22.7 us
  transfers between devices with their start and end apart: 6, of which 5 were waited for; matrix products, arithmetic and copies ran while one was open for 15% of the time, Pallas kernels for 0%

commit v1 on v0

v1 whole, which is shorter than its diff:
```python
import functools

import jax
import jax.numpy as jnp
import numpy as np
from jax import lax
from jax.experimental import pallas as pl
from jax.experimental.pallas import tpu as pltpu
from jax.sharding import PartitionSpec as P

WH = 6
WW = 12
HEADS = 8
ROWS = 24
COLS = 48
C = 512
FF = 2048
CHUNK = 512
CHUNKS = FF // CHUNK
TILE = WH * COLS
TILES = ROWS // WH
WINDOW = WH * WW
SIDE = 16
SHIFT_H = WH // 2
SHIFT_W = WW // 2
DEVICES = 128
EPS = 1e-05
MESH = pl.DeviceIdType.MESH
F32 = jnp.float32
BF16 = jnp.bfloat16
FAR = -1e30


def nn(a, b):
    return jnp.dot(a, b, preferred_element_type=F32)


def nt(a, b):
    return lax.dot_general(a, b, (((1,), (1,)), ((), ())), preferred_element_type=F32)


def window_order():
    place = np.zeros((TILE, TILE + WH * SIDE), np.float32)
    for i in range(TILE):
        w, r, c = i // WINDOW, (i % WINDOW) // WW, i % WW
        col = SHIFT_W + w * WW + c
        place[i, r * COLS + col if col < COLS else TILE + r * SIDE + col - COLS] = 1.0
    return place


def normalize(values):
    centred = values - jnp.mean(values, axis=-1, keepdims=True)
    scale = lax.rsqrt(jnp.mean(centred * centred, axis=-1, keepdims=True) + EPS)
    return centred * scale, scale


def normal_cdf(v):
    bell = jnp.exp(v * v * -0.5)
    t = 1.0 / (1.0 + jnp.abs(v) * (0.3275911 * 0.7071067811865476))
    tail = t * 0.5307027145 + -0.7265760135
    tail = tail * t + 0.7107068705
    tail = tail * t + -0.142248368
    tail = tail * t + 0.127414796
    tail = tail * t * bell
    return jnp.where(v >= 0.0, 1.0 - tail, tail), bell


def gelu(v):
    return v * normal_cdf(v)[0]


def kernel(
    comm,
    x1_hbm, x2_hbm, cot_hbm, wqkv_hbm, wout_hbm, wup_hbm, wdown_hbm,
    gain_attn, gain_mlp, bias, place, place_t,
    out_hbm, gi_hbm, gup_out, gdn_out,
    x2, cot, normed, normed_t, cot_t, back_norm, hid, bb,
    wqkv, wout, wup, wdown, biases,
    g_up, g_dn, c_up, c_dn, h_up, h_dn, a1_up, a1_dn, u1, d1, a2_up, a2_dn, u2, d2, a3_up, a3_dn,
    x1, x1_side, row_in, corner_in, out, out_side, row_back, side_back, corner_back, qkv, att,
    load_sem, store_sem, halo_send, halo_recv, back_send, back_recv,
    core_send, core_recv, s1_send, s1_recv, s2_send, s2_recv, s3_send, s3_recv,
):
    lat = lax.axis_index("lat")
    lon = lax.axis_index("lon")
    y_lo, z = lat // 4, lat % 4
    x, y_hi, core = lon // 4, (lon // 2) % 2, lon % 2
    y = y_hi * 2 + y_lo
    lat_next, lat_prev = (lat + 1) % 8, (lat + 7) % 8
    lon_next, lon_prev = (lon + 1) % 16, (lon + 15) % 16

    def core_peer():
        return (lat, lon + 1 - 2 * core)

    def x_peer(k):
        other = (x + k) % 4
        return other, (lat, other * 4 + y_hi * 2 + core)

    def z_peer(k):
        other = (z + k) % 4
        return other, (y_lo * 4 + other, lon)

    def y_peer(k):
        other = (y + k) % 4
        lo, hi = other % 2, other // 2
        return lo, hi, (lo * 4 + z, x * 4 + hi * 2 + core)

    def load(i, src, dst):
        return pltpu.make_async_copy(src, dst, load_sem.at[i])

    loads = [
        load(0, x2_hbm, x2),
        load(1, cot_hbm, cot),
        load(2, wup_hbm, wup),
        load(3, wdown_hbm, wdown),
        load(4, x1_hbm, x1.at[pl.ds(0, ROWS)]),
        load(5, wqkv_hbm, wqkv),
        load(6, wout_hbm, wout),
    ]
    for item in loads:
        item.start()

    def remote(src, dst, send, recv, device):
        return pltpu.make_async_remote_copy(
            src_ref=src, dst_ref=dst, send_sem=send, recv_sem=recv,
            device_id=device, device_id_type=MESH,
        )

    halos = [
        remote(x1_hbm.at[pl.ds(0, SHIFT_H)], row_in, halo_send.at[0], halo_recv.at[0], (lat_prev, lon)),
        remote(
            x1_hbm.at[:, pl.ds(0, SIDE)], x1_side.at[pl.ds(0, ROWS)], halo_send.at[1], halo_recv.at[1],
            (lat, lon_prev),
        ),
        remote(
            x1_hbm.at[pl.ds(0, SHIFT_H), pl.ds(0, SIDE)], corner_in, halo_send.at[2], halo_recv.at[2],
            (lat_prev, lon_prev),
        ),
    ]
    if comm:
        barrier = pltpu.get_barrier_semaphore()
        peers = [
            (lat_next, lon), (lat_prev, lon), (lat, lon_next), (lat, lon_prev),
            (lat_next, lon_next), (lat_prev, lon_prev), core_peer(),
        ]
        for k in (1, 2, 3):
            peers += [x_peer(k)[1], z_peer(k)[1], y_peer(k)[2]]
        for peer in peers:
            pl.semaphore_signal(barrier, inc=1, device_id=peer, device_id_type=MESH)
        pl.semaphore_wait(barrier, len(peers))
        for item in halos:
            item.start()

    def core_copies(j):
        other = 1 - core
        return [
            remote(g_up.at[j, other], c_up.at[j], core_send.at[j, 0], core_recv.at[j, 0], core_peer()),
            remote(g_dn.at[j, other], c_dn.at[j], core_send.at[j, 1], core_recv.at[j, 1], core_peer()),
        ]

    def first_copies(j):
        copies = []
        for k in (1, 2, 3):
            other, device = z_peer(k)
            copies.append(remote(
                h_up.at[j, :, other], a1_up.at[k - 1, j], s1_send.at[j, k - 1, 0], s1_recv.at[j, k - 1, 0], device))
            other, device = x_peer(k)
            copies.append(remote(
                h_dn.at[j, :, other], a1_dn.at[k - 1, j], s1_send.at[j, k - 1, 1], s1_recv.at[j, k - 1, 1], device))
        return copies

    def second_copies():
        copies = []
        for k in (1, 2, 3):
            other, device = x_peer(k)
            copies.append(remote(
                u1.at[:, :, other], a2_up.at[k - 1], s2_send.at[k - 1, 0], s2_recv.at[k - 1, 0], device))
            other, device = z_peer(k)
            copies.append(remote(
                d1.at[:, other], a2_dn.at[k - 1], s2_send.at[k - 1, 1], s2_recv.at[k - 1, 1], device))
        return copies

    def third_copies():
        copies = []
        for k in (1, 2, 3):
            lo, hi, device = y_peer(k)
            copies.append(remote(
                u2.at[:, lo, hi], a3_up.at[k - 1], s3_send.at[k - 1, 0], s3_recv.at[k - 1, 0], device))
            copies.append(remote(
                d2.at[lo, hi], a3_dn.at[k - 1], s3_send.at[k - 1, 1], s3_recv.at[k - 1, 1], device))
        return copies

    def core_finish(j):
        if comm:
            for item in core_copies(j):
                item.wait()
        h_up[j] = (g_up[j, core].astype(F32) + c_up[j].astype(F32)).astype(BF16).reshape(2, 4, 8, 16, 128)
        h_dn[j] = (g_dn[j, core].astype(F32) + c_dn[j].astype(F32)).astype(BF16).reshape(2, 4, 2, 16, C)
        if comm:
            for item in first_copies(j):
                item.start()

    def first_finish():
        def wait_chunk(j, carry):
            for item in first_copies(j):
                item.wait()
            return carry

        if comm:
            lax.fori_loop(0, CHUNKS, wait_chunk, 0)
        total = h_up[:, :, z].astype(F32)
        for k in range(3):
            total += a1_up[k].astype(F32)
        u1[...] = total.astype(BF16).reshape(4, 2, 4, 2, 16, 128)
        total = h_dn[:, :, x].astype(F32)
        for k in range(3):
            total += a1_dn[k].astype(F32)
        d1[...] = total.astype(BF16).reshape(2, 4, 2, 16, C)
        if comm:
            for item in second_copies():
                item.start()

    def second_finish():
        if comm:
            for item in second_copies():
                item.wait()
        total = u1[:, :, x].astype(F32)
        for k in range(3):
            total += a2_up[k].astype(F32)
        u2[...] = total.astype(BF16)
        total = d1[:, z].astype(F32)
        for k in range(3):
            total += a2_dn[k].astype(F32)
        d2[...] = total.astype(BF16)
        if comm:
            for item in third_copies():
                item.start()

    def third_finish():
        if comm:
            for item in third_copies():
                item.wait()
        total = u2[:, y_lo, y_hi].astype(F32)
        for k in range(3):
            total += a3_up[k].astype(F32)
        gup_out[...] = total * (1.0 / DEVICES)
        total = d2[y_lo, y_hi].astype(F32)
        for k in range(3):
            total += a3_dn[k].astype(F32)
        gdn_out[...] = total * (1.0 / DEVICES)

    loads[0].wait()
    loads[1].wait()

    def prepare(t, carry):
        rows = pl.ds(pl.multiple_of(t * 384, 384), 384)
        band = pl.ds(t * 8, 8)
        centred, _ = normalize(x2[band].reshape(384, C).astype(F32))
        tile = (centred * gain_mlp[...]).astype(BF16)
        normed[rows, :] = tile
        normed_t[:, rows] = tile.T
        cot_t[:, rows] = cot[band].reshape(384, C).T
        return carry

    lax.fori_loop(0, 3, prepare, 0)
    loads[2].wait()
    loads[3].wait()

    sub = lax.broadcasted_iota(jnp.int32, (64, 8, 128), 1) < 4

    def chunk_step(j, carry):
        units = pl.ds(pl.multiple_of(j * CHUNK, CHUNK), CHUNK)
        w_in = wup[:, units]
        w_back = wdown[units, :]
        for t in range(TILES):
            rows = slice(t * TILE, (t + 1) * TILE)
            before = nn(normed[rows, :], w_in)
            back_hidden = nt(cot[WH * t:WH * (t + 1)].reshape(TILE, C), w_back)
            cdf, bell = normal_cdf(before)
            hid[rows, :] = (before * cdf).astype(BF16)
            slope = cdf + before * bell * 0.3989422804014327
            back = (back_hidden * slope).astype(BF16)
            bb[rows, :] = back
            part = nt(back, w_in)
            back_norm[rows, :] = jnp.where(j == 0, part, back_norm[rows, :] + part)
        grad_up = nn(normed_t[...], bb[...])
        pieces = [grad_up[:, 128 * i:128 * (i + 1)].reshape(64, 8, 128) for i in range(4)]
        turned = [pltpu.roll(piece, 4, 1) for piece in pieces]
        for side in range(2):
            halves = []
            for i in (0, 2):
                if side == 0:
                    halves.append(jnp.where(sub, pieces[i], turned[i + 1]))
                else:
                    halves.append(jnp.where(sub, turned[i], pieces[i + 1]))
            g_up[j, side] = jnp.concatenate(halves, axis=1).astype(BF16)
        grad_down = nn(cot_t[...], hid[...]).astype(BF16).T.reshape(16, 2, 16, C)
        g_dn[j, 0] = grad_down[:, 0]
        g_dn[j, 1] = grad_down[:, 1]
        if comm:
            for item in core_copies(j):
                item.start()

        @pl.when(j >= 1)
        def _():
            core_finish(j - 1)

        return carry

    lax.fori_loop(0, CHUNKS, chunk_step, 0)

    def input_grad(t, carry):
        rows = pl.ds(pl.multiple_of(t * TILE, TILE), TILE)
        band = pl.ds(t * WH, WH)
        centred, scale = normalize(x2[band].reshape(TILE, C).astype(F32))
        back = back_norm[rows, :] * gain_mlp[...]
        mean_back = jnp.mean(back, axis=-1, keepdims=True)
        mean_both = jnp.mean(back * centred, axis=-1, keepdims=True)
        grad = cot[band].reshape(TILE, C).astype(F32) + scale * (back - mean_back - centred * mean_both)
        x2[band] = grad.astype(BF16).reshape(WH, COLS, C)
        return carry

    lax.fori_loop(0, TILES, input_grad, 0)
    store_gi = pltpu.make_async_copy(x2, gi_hbm, store_sem.at[0])
    store_gi.start()
    core_finish(CHUNKS - 1)

    loads[4].wait()
    loads[5].wait()
    loads[6].wait()
    if comm:
        for item in halos:
            item.wait()
    x1[ROWS:ROWS + SHIFT_H] = row_in[...]
    x1_side[ROWS:ROWS + SHIFT_H] = corner_in[...]
    upper_q = lax.broadcasted_iota(jnp.int32, (WINDOW, WINDOW), 0) < WINDOW // 2
    upper_k = lax.broadcasted_iota(jnp.int32, (WINDOW, WINDOW), 1) < WINDOW // 2
    split = jnp.where(upper_q == upper_k, 0.0, jnp.where(lat == 7, FAR, 0.0))
    biases[0] = bias[...]
    biases[1] = bias[...] + split[None]
    low = lax.broadcasted_iota(jnp.int32, (WINDOW, 128), 1) < 64

    def side_copy(b):
        band = pl.ds(SHIFT_H + WH * b, WH)
        return remote(
            out_side.at[band], side_back.at[band], back_send.at[b], back_recv.at[b], (lat, lon_next))

    def far_copies():
        tail = pl.ds(ROWS, SHIFT_H)
        return [
            remote(out.at[tail], row_back, back_send.at[4], back_recv.at[4], (lat_next, lon)),
            remote(out_side.at[tail], corner_back, back_send.at[5], back_recv.at[5], (lat_next, lon_next)),
        ]

    def band_step(step, carry):
        b = TILES - 1 - step
        band = pl.ds(SHIFT_H + WH * b, WH)
        cells = jnp.concatenate(
            [x1[band].reshape(TILE, C), x1_side[band].reshape(WH * SIDE, C)], axis=0)
        tokens = nn(place[...], cells)
        centred, _ = normalize(tokens)
        qkv[...] = nn((centred * gain_attn[...]).astype(BF16), wqkv[...])
        masked = jnp.where(b == TILES - 1, 1, 0)

        def window_step(w, inner):
            rows = pl.ds(pl.multiple_of(w * WINDOW, 8), WINDOW)
            for pair in range(HEADS // 2):
                lanes = slice(128 * pair, 128 * (pair + 1))
                query = (qkv[rows, 128 * pair:128 * pair + 128] * 0.125).astype(BF16)
                key = qkv[rows, C + 128 * pair:C + 128 * pair + 128]
                value = qkv[rows, 2 * C + 128 * pair:2 * C + 128 * pair + 128]
                blended = []
                for side in range(2):
                    mine = low if side == 0 else jnp.logical_not(low)
                    scores = nt(query, jnp.where(mine, key, 0.0).astype(BF16))
                    scores = scores + biases[masked, 2 * pair + side]
                    raised = jnp.exp(scores - jnp.max(scores, axis=-1, keepdims=True)).astype(BF16)
                    blended.append(nn(raised, jnp.where(mine, value, 1.0).astype(BF16)))
                sums = pltpu.roll(jnp.where(low, blended[1], blended[0]), 64, 1)
                att[rows, lanes] = jnp.where(low, blended[0], blended[1]) / sums
            return inner

        lax.fori_loop(0, TILE // WINDOW, window_step, 0)
        residual = tokens + nn(att[...].astype(BF16), wout[...])
        mid, _ = normalize(residual)
        mid = (mid * gain_mlp[...]).astype(BF16)
        total = residual
        for j in range(CHUNKS):
            units = slice(j * CHUNK, (j + 1) * CHUNK)
            hidden = gelu(nn(mid, wup[:, units])).astype(BF16)
            total = total + nn(hidden, wdown[units, :])
        cells = nn(place_t[...], total.astype(BF16)).astype(BF16)
        out[band] = cells[:TILE].reshape(WH, COLS, C)
        out_side[band] = cells[TILE:].reshape(WH, SIDE, C)
        if comm:
            side_copy(b).start()

        @pl.when(step == 0)
        def _():
            if comm:
                for item in far_copies():
                    item.start()
            first_finish()

        @pl.when(step == 1)
        def _():
            second_finish()

        @pl.when(step == 2)
        def _():
            third_finish()

        return carry

    lax.fori_loop(0, TILES, band_step, 0)
    if comm:
        for item in far_copies():
            item.wait()
        for b in range(TILES):
            side_copy(b).wait()
    inside = pl.ds(SHIFT_H, ROWS - SHIFT_H)
    out[inside, pl.ds(0, SIDE)] = out[inside, pl.ds(0, SIDE)] + side_back[inside]
    out[0:SHIFT_H] = row_back[...]
    out[0:SHIFT_H, 0:SIDE] = out[0:SHIFT_H, 0:SIDE] + corner_back[...]
    store_out = pltpu.make_async_copy(out.at[pl.ds(0, ROWS)], out_hbm, store_sem.at[1])
    store_out.start()
    store_gi.wait()
    store_out.wait()


def scratch():
    v = pltpu.VMEM
    tokens = ROWS * COLS
    ext = ROWS + SHIFT_H
    dma = pltpu.SemaphoreType.DMA
    return [
        v((ROWS, COLS, C), BF16), v((ROWS, COLS, C), BF16), v((tokens, C), BF16), v((C, tokens), BF16),
        v((C, tokens), BF16), v((tokens, C), F32), v((tokens, CHUNK), BF16), v((tokens, CHUNK), BF16),
        v((C, 3 * C), BF16), v((C, C), BF16), v((C, FF), BF16), v((FF, C), BF16),
        v((2, HEADS, WINDOW, WINDOW), F32),
        v((CHUNKS, 2, 64, 16, 128), BF16), v((CHUNKS, 2, 16, 16, C), BF16),
        v((CHUNKS, 64, 16, 128), BF16), v((CHUNKS, 16, 16, C), BF16),
        v((CHUNKS, 2, 4, 8, 16, 128), BF16), v((CHUNKS, 2, 4, 2, 16, C), BF16),
        v((3, CHUNKS, 2, 8, 16, 128), BF16), v((3, CHUNKS, 2, 2, 16, C), BF16),
        v((CHUNKS, 2, 4, 2, 16, 128), BF16), v((2, 4, 2, 16, C), BF16),
        v((3, CHUNKS, 2, 2, 16, 128), BF16), v((3, 2, 2, 16, C), BF16),
        v((CHUNKS, 2, 2, 16, 128), BF16), v((2, 2, 16, C), BF16),
        v((3, CHUNKS, 16, 128), BF16), v((3, 16, C), BF16),
        v((ext, COLS, C), BF16), v((ext, SIDE, C), BF16), v((SHIFT_H, COLS, C), BF16),
        v((SHIFT_H, SIDE, C), BF16), v((ext, COLS, C), BF16), v((ext, SIDE, C), BF16),
        v((SHIFT_H, COLS, C), BF16), v((ext, SIDE, C), BF16), v((SHIFT_H, SIDE, C), BF16),
        v((TILE, 3 * C), F32), v((TILE, C), F32),
        dma((7,)), dma((2,)), dma((3,)), dma((3,)), dma((6,)), dma((6,)),
        dma((CHUNKS, 2)), dma((CHUNKS, 2)), dma((CHUNKS, 3, 2)), dma((CHUNKS, 3, 2)),
        dma((3, 2)), dma((3, 2)), dma((3, 2)), dma((3, 2)),
    ]


def shards(comm, x_first, x_second, cotangent, gain_attn, gain_mlp, w_qkv, w_out, w_up, w_down, bias):
    place = window_order()
    anywhere = pl.BlockSpec(memory_space=pl.ANY)
    near = pl.BlockSpec(memory_space=pltpu.VMEM)
    params = dict(vmem_limit_bytes=60 * 1024 * 1024, has_side_effects=True)
    if comm:
        params["collective_id"] = 0
    out_first, grad_input, up, down = pl.pallas_call(
        functools.partial(kernel, comm),
        out_shape=(
            jax.ShapeDtypeStruct((ROWS, COLS, C), BF16),
            jax.ShapeDtypeStruct((ROWS, COLS, C), BF16),
            jax.ShapeDtypeStruct((CHUNKS, 16, 128), F32),
            jax.ShapeDtypeStruct((16, C), F32),
        ),
        in_specs=[anywhere] * 7 + [near] * 5,
        out_specs=(anywhere, anywhere, near, near),
        scratch_shapes=scratch(),
        compiler_params=pltpu.CompilerParams(**params),
        cost_estimate=pl.CostEstimate(flops=20 * 10**9, bytes_accessed=13 * 10**6, transcendentals=10**7),
        name="swin_block",
    )(
        x_first, x_second, cotangent, w_qkv, w_out, w_up, w_down,
        gain_attn.reshape(1, C), gain_mlp.reshape(1, C), bias,
        jnp.asarray(place, BF16), jnp.asarray(place.T, BF16),
    )
    up = up.reshape(4, 4, 4, 128).transpose(2, 0, 1, 3).reshape(4, FF)
    return out_first, grad_input, up, down


def solution(mesh):
    cells = P("lat", "lon", None)
    return jax.shard_map(
        functools.partial(shards, True),
        mesh=mesh,
        in_specs=(cells, cells, cells) + (P(),) * 7,
        out_specs=(cells, cells, P(("lat", "lon"), None), P(("lat", "lon"), None)),
        check_vma=False,
    )
```

time: 844 us -> 77.8 us (0.09)
  the two profiles are of different devices: /device:TPU:1 before, /device:TPU:0 now
where the time goes in v1:
time: 77.8 us; the launch traced here: 77.6 us
  Pallas kernels  72.3 us (93%)
  local copies, waits for them, and re-layouts  4.71 us (6%)
    pallas_call x1, Pallas kernels, shards(): pl.pallas_call(functools.partial(kernel, comm), out_shape=(jax.ShapeDtype...  72.3 us
    unnamed x10, local copies, waits for them, and re-layouts  4.71 us

profile of v1, /device:TPU:0, one launch (start us, length us, event | category | flops | bytes accessed | tf_op | source)
XLA Modules:
  0.0 77.6 jit_solution(5779741570689817215)
XLA Ops:
  0.6 72.3 %swin_block.1 = (bf16[24,48,512]{2,1,0:T(8,128)(2,1)}, bf16[24,48,512]{2,1,0:T(8,128)(2,1)}, f32[4,16,128]{2,1,0:T(8,128)}, f32[16,512]{1,0:T(8,128)}) custom-call(bf16[24,48,512]{2,1,0:T(8,128)(2,1)} %x1_hbm.1, bf16[24,48,512]{2,1,0:T(8,128)(2,1)} %x2_hbm.1, bf16[24,48,512]{2,1,0:T(8,128)(2,1)} %cot_hbm.1, bf16[512,1536]{1,0:T(8,128)(2,1)} %wqkv_hbm.1, ...), custom_call_target="tpu_custom_call" | custom-call | flops 20000000000 | bytes 13000000 | tf_op jit(solution)/shard_map/swin_block/pallas_call | solution.py:466
  72.9 0.0 copy-start
  72.9 2.5 %copy.21 = bf16[24,48,512]{2,1,0:T(8,128)(2,1)} copy(bf16[24,48,512]{2,1,0:T(8,128)(2,1)} %get-tuple-element.16) | data formatting | bytes 2359296
  75.4 0.0 copy-done
  75.4 0.0 copy-start.2
  75.4 0.0 copy-start.1
  75.4 1.0 %copy.22 = bf16[24,48,512]{2,1,0:T(8,128)(2,1)} copy(bf16[24,48,512]{2,1,0:T(8,128)(2,1)S(1)} %copy-done) | data formatting | bytes 2359296
  76.4 0.0 copy-done.2
  76.4 0.6 copy.23
  77.0 0.0 copy-done.1
  77.0 0.6 copy.24
Async XLA Ops:
  72.9 2.5 %copy-start = (bf16[24,48,512]{2,1,0:T(8,128)(2,1)S(1)}, bf16[24,48,512]{2,1,0:T(8,128)(2,1)}, u32[]{:S(2)}) copy-start(bf16[24,48,512]{2,1,0:T(8,128)(2,1)} %get-tuple-element.17) | copy-start | bytes 3538948
  75.4 1.0 %copy-start.2 = (f32[4,16,128]{2,1,0:T(8,128)S(1)}, f32[4,16,128]{2,1,0:T(8,128)}, u32[]{:S(2)}) copy-start(f32[4,16,128]{2,1,0:T(8,128)} %get-tuple-element.10) | copy-start | bytes 98308
  75.4 1.6 %copy-start.1 = (f32[16,512]{1,0:T(8,128)S(1)}, f32[16,512]{1,0:T(8,128)}, u32[]{:S(2)}) copy-start(f32[16,512]{1,0:T(8,128)} %get-tuple-element.19) | copy-start | bytes 98308

commit v2 on v1

--- a/solution.py
+++ b/solution.py
@@ -18,8 +18,12 @@
 CHUNK = 512
 CHUNKS = FF // CHUNK
 TILE = WH * COLS
+HALF = ROWS * COLS // 2
 TILES = ROWS // WH
+INNER = TILES - 1
 WINDOW = WH * WW
+EDGE = TILES + INNER
+LAST = INNER * WH + WH // 2
 SIDE = 16
 SHIFT_H = WH // 2
 SHIFT_W = WW // 2
@@ -39,13 +43,23 @@
     return lax.dot_general(a, b, (((1,), (1,)), ((), ())), preferred_element_type=F32)
 
 
-def window_order():
-    place = np.zeros((TILE, TILE + WH * SIDE), np.float32)
-    for i in range(TILE):
-        w, r, c = i // WINDOW, (i % WINDOW) // WW, i % WW
-        col = SHIFT_W + w * WW + c
-        place[i, r * COLS + col if col < COLS else TILE + r * SIDE + col - COLS] = 1.0
+def one_hot(windows, rows, first_col, own_cols, side_cols):
+    place = np.zeros((len(windows) * WINDOW, rows * (own_cols + side_cols)), np.float32)
+    for n, (row, col) in enumerate(windows):
+        for i in range(WINDOW):
+            r, c = row + i // WW, col + i % WW
+            at = r * own_cols + c - first_col if c < COLS else rows * own_cols + r * side_cols + c - COLS
+            place[n * WINDOW + i, at] = 1.0
     return place
+
+
+def window_orders():
+    starts = [SHIFT_W + WW * w for w in range(COLS // WW)]
+    return [
+        one_hot([(0, col) for col in starts], WH, 0, COLS, SIDE),
+        one_hot([(WH * b, starts[-1]) for b in range(INNER)], INNER * WH, COLS - SIDE, SIDE, SIDE),
+        one_hot([(0, col) for col in starts[:-1]], WH, 0, COLS, 0),
+    ]
 
 
 def normalize(values):
@@ -55,29 +69,22 @@
 
 
 def normal_cdf(v):
-    bell = jnp.exp(v * v * -0.5)
-    t = 1.0 / (1.0 + jnp.abs(v) * (0.3275911 * 0.7071067811865476))
-    tail = t * 0.5307027145 + -0.7265760135
-    tail = tail * t + 0.7107068705
-    tail = tail * t + -0.142248368
-    tail = tail * t + 0.127414796
-    tail = tail * t * bell
-    return jnp.where(v >= 0.0, 1.0 - tail, tail), bell
+    return 0.5 + 0.5 * lax.erf(v * 0.7071067811865476)
 
 
 def gelu(v):
-    return v * normal_cdf(v)[0]
+    return v * normal_cdf(v)
 
 
 def kernel(
     comm,
     x1_hbm, x2_hbm, cot_hbm, wqkv_hbm, wout_hbm, wup_hbm, wdown_hbm,
-    gain_attn, gain_mlp, bias, place, place_t,
+    gain_attn, gain_mlp, bias, p_last, p_side, p_inner, q_last, q_side, q_inner,
     out_hbm, gi_hbm, gup_out, gdn_out,
     x2, cot, normed, normed_t, cot_t, back_norm, hid, bb,
     wqkv, wout, wup, wdown, biases,
     g_up, g_dn, c_up, c_dn, h_up, h_dn, a1_up, a1_dn, u1, d1, a2_up, a2_dn, u2, d2, a3_up, a3_dn,
-    x1, x1_side, row_in, corner_in, out, out_side, row_back, side_back, corner_back, qkv, att,
+    x1, x1_side, row_in, corner_in, out, out_side, row_back, side_back, corner_back, tokens, padded, wqv_t, q_t, v_t, keys, att_t,
     load_sem, store_sem, halo_send, halo_recv, back_send, back_recv,
     core_send, core_recv, s1_send, s1_recv, s2_send, s2_recv, s3_send, s3_recv,
 ):
@@ -147,6 +154,8 @@
             peers += [x_peer(k)[1], z_peer(k)[1], y_peer(k)[2]]
         for peer in peers:
             pl.semaphore_signal(barrier, inc=1, device_id=peer, device_id_type=MESH)
+
+    def meet():
         pl.semaphore_wait(barrier, len(peers))
         for item in halos:
             item.start()
@@ -243,7 +252,9 @@
         total = u2[:, y_lo, y_hi].astype(F32)
         for k in range(3):
             total += a3_up[k].astype(F32)
-        gup_out[...] = total * (1.0 / DEVICES)
+        for j in range(CHUNKS):
+            for i in range(4):
+                gup_out[:, CHUNK * j + 128 * i:CHUNK * j + 128 * (i + 1)] = total[j, 4 * i:4 * (i + 1)] * (1.0 / DEVICES)
         total = d2[y_lo, y_hi].astype(F32)
         for k in range(3):
             total += a3_dn[k].astype(F32)
@@ -272,13 +283,13 @@
         units = pl.ds(pl.multiple_of(j * CHUNK, CHUNK), CHUNK)
         w_in = wup[:, units]
         w_back = wdown[units, :]
-        for t in range(TILES):
-            rows = slice(t * TILE, (t + 1) * TILE)
+        for t in range(2):
+            rows = slice(t * HALF, (t + 1) * HALF)
             before = nn(normed[rows, :], w_in)
-            back_hidden = nt(cot[WH * t:WH * (t + 1)].reshape(TILE, C), w_back)
-            cdf, bell = normal_cdf(before)
+            back_hidden = nt(cot[12 * t:12 * (t + 1)].reshape(HALF, C), w_back)
+            cdf = normal_cdf(before)
             hid[rows, :] = (before * cdf).astype(BF16)
-            slope = cdf + before * bell * 0.3989422804014327
+            slope = cdf + before * (jnp.exp(before * before * -0.5) * 0.3989422804014327)
             back = (back_hidden * slope).astype(BF16)
             bb[rows, :] = back
             part = nt(back, w_in)
@@ -298,6 +309,7 @@
         g_dn[j, 0] = grad_down[:, 0]
         g_dn[j, 1] = grad_down[:, 1]
         if comm:
+            pl.when(j == 0)(meet)
             for item in core_copies(j):
                 item.start()
 
@@ -336,52 +348,51 @@
     upper_q = lax.broadcasted_iota(jnp.int32, (WINDOW, WINDOW), 0) < WINDOW // 2
     upper_k = lax.broadcasted_iota(jnp.int32, (WINDOW, WINDOW), 1) < WINDOW // 2
     split = jnp.where(upper_q == upper_k, 0.0, jnp.where(lat == 7, FAR, 0.0))
-    biases[0] = bias[...]
-    biases[1] = bias[...] + split[None]
-    low = lax.broadcasted_iota(jnp.int32, (WINDOW, 128), 1) < 64
-
-    def side_copy(b):
-        band = pl.ds(SHIFT_H + WH * b, WH)
-        return remote(
-            out_side.at[band], side_back.at[band], back_send.at[b], back_recv.at[b], (lat, lon_next))
-
-    def far_copies():
-        tail = pl.ds(ROWS, SHIFT_H)
-        return [
-            remote(out.at[tail], row_back, back_send.at[4], back_recv.at[4], (lat_next, lon)),
-            remote(out_side.at[tail], corner_back, back_send.at[5], back_recv.at[5], (lat_next, lon_next)),
-        ]
-
-    def band_step(step, carry):
-        b = TILES - 1 - step
-        band = pl.ds(SHIFT_H + WH * b, WH)
-        cells = jnp.concatenate(
-            [x1[band].reshape(TILE, C), x1_side[band].reshape(WH * SIDE, C)], axis=0)
-        tokens = nn(place[...], cells)
-        centred, _ = normalize(tokens)
-        qkv[...] = nn((centred * gain_attn[...]).astype(BF16), wqkv[...])
-        masked = jnp.where(b == TILES - 1, 1, 0)
-
-        def window_step(w, inner):
-            rows = pl.ds(pl.multiple_of(w * WINDOW, 8), WINDOW)
-            for pair in range(HEADS // 2):
-                lanes = slice(128 * pair, 128 * (pair + 1))
-                query = (qkv[rows, 128 * pair:128 * pair + 128] * 0.125).astype(BF16)
-                key = qkv[rows, C + 128 * pair:C + 128 * pair + 128]
-                value = qkv[rows, 2 * C + 128 * pair:2 * C + 128 * pair + 128]
-                blended = []
-                for side in range(2):
-                    mine = low if side == 0 else jnp.logical_not(low)
-                    scores = nt(query, jnp.where(mine, key, 0.0).astype(BF16))
-                    scores = scores + biases[masked, 2 * pair + side]
-                    raised = jnp.exp(scores - jnp.max(scores, axis=-1, keepdims=True)).astype(BF16)
-                    blended.append(nn(raised, jnp.where(mine, value, 1.0).astype(BF16)))
-                sums = pltpu.roll(jnp.where(low, blended[1], blended[0]), 64, 1)
-                att[rows, lanes] = jnp.where(low, blended[0], blended[1]) / sums
-            return inner
-
-        lax.fori_loop(0, TILE // WINDOW, window_step, 0)
-        residual = tokens + nn(att[...].astype(BF16), wout[...])
+    biases[...] = jnp.zeros(biases.shape, F32)
+    for head in range(HEADS):
+        lanes = pl.ds(128 * (head % 2), WINDOW)
+        turned = bias[head].T
+        biases[0, head // 2, :, lanes] = turned
+        biases[1, head // 2, :, lanes] = turned + split
+    padded[...] = jnp.zeros(padded.shape, BF16)
+    wqv_t[0:C] = wqkv[:, 0:C].T
+    wqv_t[C:2 * C] = wqkv[:, 2 * C:3 * C].T
+    upper = lax.broadcasted_iota(jnp.int32, (128, 128), 0) < 64
+    nothing = jnp.zeros((128, 128), BF16)
+    gap = jnp.zeros((128 - WINDOW, 256), BF16)
+
+    def project(windows):
+        centred, _ = normalize(tokens[0:windows * WINDOW])
+        centred = centred * gain_attn[...]
+        for w in range(windows):
+            padded[128 * w:128 * w + WINDOW] = centred[WINDOW * w:WINDOW * (w + 1)].astype(BF16)
+        cells = padded[0:128 * windows]
+        q_t[:, 0:128 * windows] = (nt(wqv_t[0:C], cells) * 0.125).astype(BF16)
+        v_t[:, 0:128 * windows] = nt(wqv_t[C:2 * C], cells).astype(BF16)
+        keys[0:128 * windows] = nn(cells, wqkv[:, C:2 * C]).astype(BF16)
+
+    def attend(masks):
+        def pair_step(pair, carry):
+            heads = pl.ds(pl.multiple_of(pair * 128, 128), 128)
+            for w, masked in enumerate(masks):
+                cells = slice(w * 128, (w + 1) * 128)
+                query = q_t[heads, cells]
+                query = jnp.concatenate(
+                    [jnp.where(upper, query, nothing), jnp.where(upper, nothing, query)], axis=1)
+                scores = nn(keys[w * 128:w * 128 + WINDOW, heads], query) + biases[masked, pair]
+                raised = jnp.exp(scores - jnp.max(scores, axis=0, keepdims=True))
+                inverse = 1.0 / jnp.sum(raised, axis=0, keepdims=True)
+                blended = nn(v_t[heads, cells], jnp.concatenate([raised.astype(BF16), gap], axis=0)) * inverse
+                att_t[heads, cells] = jnp.where(upper, blended[:, :128], blended[:, 128:]).astype(BF16)
+            return carry
+
+        lax.fori_loop(0, HEADS // 2, pair_step, 0)
+
+    def feed_forward(windows):
+        mixed = lax.dot_general(
+            att_t[:, 0:128 * windows], wout[...], (((0,), (0,)), ((), ())), preferred_element_type=F32)
+        mixed = jnp.concatenate([mixed[128 * w:128 * w + WINDOW] for w in range(windows)], axis=0)
+        residual = tokens[0:windows * WINDOW] + mixed
         mid, _ = normalize(residual)
         mid = (mid * gain_mlp[...]).astype(BF16)
         total = residual
@@ -389,39 +400,60 @@
             units = slice(j * CHUNK, (j + 1) * CHUNK)
             hidden = gelu(nn(mid, wup[:, units])).astype(BF16)
             total = total + nn(hidden, wdown[units, :])
-        cells = nn(place_t[...], total.astype(BF16)).astype(BF16)
-        out[band] = cells[:TILE].reshape(WH, COLS, C)
-        out_side[band] = cells[TILE:].reshape(WH, SIDE, C)
-        if comm:
-            side_copy(b).start()
-
-        @pl.when(step == 0)
-        def _():
-            if comm:
-                for item in far_copies():
-                    item.start()
-            first_finish()
-
-        @pl.when(step == 1)
-        def _():
-            second_finish()
-
-        @pl.when(step == 2)
-        def _():
-            third_finish()
-
-        return carry
-
-    lax.fori_loop(0, TILES, band_step, 0)
+        return total
+
+    above = pl.ds(SHIFT_H, INNER * WH)
+    last = pl.ds(LAST, WH)
+    tail = pl.ds(ROWS, SHIFT_H)
+    right = pl.ds(COLS - SIDE, SIDE)
+    cells = jnp.concatenate([x1[last].reshape(TILE, C), x1_side[last].reshape(WH * SIDE, C)], axis=0)
+    tokens[0:TILE] = nn(p_last[...], cells)
+    cells = jnp.concatenate(
+        [x1[above, right].reshape(INNER * WH * SIDE, C), x1_side[above].reshape(INNER * WH * SIDE, C)], axis=0)
+    tokens[TILE:EDGE * WINDOW] = nn(p_side[...], cells)
+    project(EDGE)
+    attend([1] * TILES + [0] * INNER)
+    first_finish()
+    total = feed_forward(EDGE)
+    cells = nn(q_last[...], total[:TILE].astype(BF16)).astype(BF16)
+    out[last] = cells[:TILE].reshape(WH, COLS, C)
+    out_side[last] = cells[TILE:].reshape(WH, SIDE, C)
+    cells = nn(q_side[...], total[TILE:].astype(BF16)).astype(BF16)
+    out[above, right] = cells[:INNER * WH * SIDE].reshape(INNER * WH, SIDE, C)
+    out_side[above] = cells[INNER * WH * SIDE:].reshape(INNER * WH, SIDE, C)
+    inside = pl.ds(SHIFT_H, ROWS - SHIFT_H)
+    returns = [
+        remote(out.at[tail], row_back, back_send.at[0], back_recv.at[0], (lat_next, lon)),
+        remote(out_side.at[inside], side_back.at[inside], back_send.at[1], back_recv.at[1], (lat, lon_next)),
+        remote(out_side.at[tail], corner_back, back_send.at[2], back_recv.at[2], (lat_next, lon_next)),
+    ]
     if comm:
-        for item in far_copies():
+        for item in returns:
+            item.start()
+    second_finish()
+
+    for b in range(INNER):
+        band = pl.ds(SHIFT_H + WH * b, WH)
+        rows = slice(INNER * WINDOW * b, INNER * WINDOW * (b + 1))
+        tokens[rows] = nn(p_inner[...], x1[band].reshape(TILE, C))
+    project(INNER * INNER)
+    attend([0] * (INNER * INNER))
+    third_finish()
+    total = feed_forward(INNER * INNER)
+    for b in range(INNER):
+        band = pl.ds(SHIFT_H + WH * b, WH)
+        rows = slice(INNER * WINDOW * b, INNER * WINDOW * (b + 1))
+        cells = nn(q_inner[...], total[rows].astype(BF16)).astype(BF16).reshape(WH, COLS, C)
+        out[band, pl.ds(0, COLS - SIDE)] = cells[:, :COLS - SIDE]
+        out[band, right] = out[band, right] + cells[:, COLS - SIDE:]
+
+    if comm:
+        for item in returns:
             item.wait()
-        for b in range(TILES):
-            side_copy(b).wait()
-    inside = pl.ds(SHIFT_H, ROWS - SHIFT_H)
-    out[inside, pl.ds(0, SIDE)] = out[inside, pl.ds(0, SIDE)] + side_back[inside]
+    left = pl.ds(0, SIDE)
+    out[inside, left] = out[inside, left] + side_back[inside]
     out[0:SHIFT_H] = row_back[...]
-    out[0:SHIFT_H, 0:SIDE] = out[0:SHIFT_H, 0:SIDE] + corner_back[...]
+    out[0:SHIFT_H, left] = out[0:SHIFT_H, left] + corner_back[...]
     store_out = pltpu.make_async_copy(out.at[pl.ds(0, ROWS)], out_hbm, store_sem.at[1])
     store_out.start()
     store_gi.wait()
@@ -432,12 +464,13 @@
     v = pltpu.VMEM
     tokens = ROWS * COLS
     ext = ROWS + SHIFT_H
+    wide = INNER * INNER * 128
     dma = pltpu.SemaphoreType.DMA
     return [
         v((ROWS, COLS, C), BF16), v((ROWS, COLS, C), BF16), v((tokens, C), BF16), v((C, tokens), BF16),
         v((C, tokens), BF16), v((tokens, C), F32), v((tokens, CHUNK), BF16), v((tokens, CHUNK), BF16),
         v((C, 3 * C), BF16), v((C, C), BF16), v((C, FF), BF16), v((FF, C), BF16),
-        v((2, HEADS, WINDOW, WINDOW), F32),
+        v((2, HEADS // 2, WINDOW, 256), F32),
         v((CHUNKS, 2, 64, 16, 128), BF16), v((CHUNKS, 2, 16, 16, C), BF16),
         v((CHUNKS, 64, 16, 128), BF16), v((CHUNKS, 16, 16, C), BF16),
         v((CHUNKS, 2, 4, 8, 16, 128), BF16), v((CHUNKS, 2, 4, 2, 16, C), BF16),
@@ -449,15 +482,16 @@
         v((ext, COLS, C), BF16), v((ext, SIDE, C), BF16), v((SHIFT_H, COLS, C), BF16),
         v((SHIFT_H, SIDE, C), BF16), v((ext, COLS, C), BF16), v((ext, SIDE, C), BF16),
         v((SHIFT_H, COLS, C), BF16), v((ext, SIDE, C), BF16), v((SHIFT_H, SIDE, C), BF16),
-        v((TILE, 3 * C), F32), v((TILE, C), F32),
-        dma((7,)), dma((2,)), dma((3,)), dma((3,)), dma((6,)), dma((6,)),
+        v((INNER * INNER * WINDOW, C), F32),
+        v((wide, C), BF16), v((2 * C, C), BF16), v((C, wide), BF16), v((C, wide), BF16), v((wide, C), BF16), v((C, wide), BF16),
+        dma((7,)), dma((2,)), dma((3,)), dma((3,)), dma((3,)), dma((3,)),
         dma((CHUNKS, 2)), dma((CHUNKS, 2)), dma((CHUNKS, 3, 2)), dma((CHUNKS, 3, 2)),
         dma((3, 2)), dma((3, 2)), dma((3, 2)), dma((3, 2)),
     ]
 
 
 def shards(comm, x_first, x_second, cotangent, gain_attn, gain_mlp, w_qkv, w_out, w_up, w_down, bias):
-    place = window_order()
+    places = window_orders()
     anywhere = pl.BlockSpec(memory_space=pl.ANY)
     near = pl.BlockSpec(memory_space=pltpu.VMEM)
     params = dict(vmem_limit_bytes=60 * 1024 * 1024, has_side_effects=True)
@@ -468,10 +502,10 @@
         out_shape=(
             jax.ShapeDtypeStruct((ROWS, COLS, C), BF16),
             jax.ShapeDtypeStruct((ROWS, COLS, C), BF16),
-            jax.ShapeDtypeStruct((CHUNKS, 16, 128), F32),
+            jax.ShapeDtypeStruct((4, FF), F32),
             jax.ShapeDtypeStruct((16, C), F32),
         ),
-        in_specs=[anywhere] * 7 + [near] * 5,
+        in_specs=[anywhere] * 7 + [near] * 9,
         out_specs=(anywhere, anywhere, near, near),
         scratch_shapes=scratch(),
         compiler_params=pltpu.CompilerParams(**params),
@@ -480,9 +514,8 @@
     )(
         x_first, x_second, cotangent, w_qkv, w_out, w_up, w_down,
         gain_attn.reshape(1, C), gain_mlp.reshape(1, C), bias,
-        jnp.asarray(place, BF16), jnp.asarray(place.T, BF16),
+        *[jnp.asarray(place, BF16) for place in places], *[jnp.asarray(place.T, BF16) for place in places],
     )
-    up = up.reshape(4, 4, 4, 128).transpose(2, 0, 1, 3).reshape(4, FF)
     return out_first, grad_input, up, down
 
 

time: 77.8 us -> 57.8 us (0.74)
  the two profiles are of different devices: /device:TPU:0 before, /device:TPU:1 now
where the time goes in v2:
time: 57.8 us; the launch traced here: 57.6 us
  Pallas kernels  52.3 us (90%)
  local copies, waits for them, and re-layouts  4.71 us (8%)
  between operations  0.66 us (1%)
    pallas_call x1, Pallas kernels, shards(): pl.pallas_call(functools.partial(kernel, comm), out_shape=(jax.ShapeDtype...  52.3 us
    unnamed x10, local copies, waits for them, and re-layouts  4.71 us

profile of v2, /device:TPU:1, one launch (start us, length us, event | category | flops | bytes accessed | tf_op | source)
XLA Modules:
  0.0 57.6 jit_solution(9965975657847219189)
XLA Ops:
  0.6 52.3 %swin_block.1 = (bf16[24,48,512]{2,1,0:T(8,128)(2,1)}, bf16[24,48,512]{2,1,0:T(8,128)(2,1)}, f32[4,2048]{1,0:T(4,128)}, f32[16,512]{1,0:T(8,128)}) custom-call(bf16[24,48,512]{2,1,0:T(8,128)(2,1)} %x1_hbm.1, bf16[24,48,512]{2,1,0:T(8,128)(2,1)} %x2_hbm.1, bf16[24,48,512]{2,1,0:T(8,128)(2,1)} %cot_hbm.1, bf16[512,1536]{1,0:T(8,128)(2,1)} %wqkv_hbm.1, ...), custom_call_target="tpu_custom_call" | custom-call | flops 20000000000 | bytes 13000000 | tf_op jit(solution)/shard_map/swin_block/pallas_call | solution.py:500
  52.9 0.0 copy-start
  52.9 2.5 %copy.24 = bf16[24,48,512]{2,1,0:T(8,128)(2,1)} copy(bf16[24,48,512]{2,1,0:T(8,128)(2,1)} %get-tuple-element.8) | data formatting | bytes 2359296
  55.4 0.0 copy-done
  55.4 0.0 copy-start.2
  55.4 0.0 copy-start.1
  55.4 1.0 %copy.25 = bf16[24,48,512]{2,1,0:T(8,128)(2,1)} copy(bf16[24,48,512]{2,1,0:T(8,128)(2,1)S(1)} %copy-done) | data formatting | bytes 2359296
  56.4 0.0 copy-done.2
  56.4 0.6 %copy.26 = f32[4,2048]{1,0:T(4,128)} copy(f32[4,2048]{1,0:T(4,128)S(1)} %copy-done.2) | data formatting | bytes 65536
  57.0 0.0 copy-done.1
  57.0 0.6 %copy.27 = f32[16,512]{1,0:T(8,128)} copy(f32[16,512]{1,0:T(8,128)S(1)} %copy-done.1) | data formatting | bytes 65536
Async XLA Ops:
  52.9 2.5 %copy-start = (bf16[24,48,512]{2,1,0:T(8,128)(2,1)S(1)}, bf16[24,48,512]{2,1,0:T(8,128)(2,1)}, u32[]{:S(2)}) copy-start(bf16[24,48,512]{2,1,0:T(8,128)(2,1)} %get-tuple-element.9) | copy-start | bytes 3538948
  55.4 1.0 %copy-start.2 = (f32[4,2048]{1,0:T(4,128)S(1)}, f32[4,2048]{1,0:T(4,128)}, u32[]{:S(2)}) copy-start(f32[4,2048]{1,0:T(4,128)} %get-tuple-element.10) | copy-start | bytes 98308
  55.4 1.6 %copy-start.1 = (f32[16,512]{1,0:T(8,128)S(1)}, f32[16,512]{1,0:T(8,128)}, u32[]{:S(2)}) copy-start(f32[16,512]{1,0:T(8,128)} %get-tuple-element.11) | copy-start | bytes 98308

commit v3 on v2

--- a/solution.py
+++ b/solution.py
@@ -44,7 +44,7 @@
 
 
 def one_hot(windows, rows, first_col, own_cols, side_cols):
-    place = np.zeros((len(windows) * WINDOW, rows * (own_cols + side_cols)), np.float32)
+    place = np.zeros((-(-len(windows) * WINDOW // 16) * 16, rows * (own_cols + side_cols)), np.float32)
     for n, (row, col) in enumerate(windows):
         for i in range(WINDOW):
             r, c = row + i // WW, col + i % WW
@@ -55,11 +55,12 @@
 
 def window_orders():
     starts = [SHIFT_W + WW * w for w in range(COLS // WW)]
-    return [
+    places = [
         one_hot([(0, col) for col in starts], WH, 0, COLS, SIDE),
         one_hot([(WH * b, starts[-1]) for b in range(INNER)], INNER * WH, COLS - SIDE, SIDE, SIDE),
         one_hot([(0, col) for col in starts[:-1]], WH, 0, COLS, 0),
     ]
+    return places + [place.T[:, :count * WINDOW] for place, count in zip(places, (TILES, INNER, INNER))]
 
 
 def normalize(values):
@@ -79,13 +80,13 @@
 def kernel(
     comm,
     x1_hbm, x2_hbm, cot_hbm, wqkv_hbm, wout_hbm, wup_hbm, wdown_hbm,
-    gain_attn, gain_mlp, bias, p_last, p_side, p_inner, q_last, q_side, q_inner,
-    out_hbm, gi_hbm, gup_out, gdn_out,
+    bias_hbm, p_last_hbm, p_side_hbm, p_inner_hbm, q_last_hbm, q_side_hbm, q_inner_hbm, gain_attn, gain_mlp,
+    out, gi, gup_out, gdn_out,
     x2, cot, normed, normed_t, cot_t, back_norm, hid, bb,
-    wqkv, wout, wup, wdown, biases,
+    wqkv, wout, wup, wdown, bias, p_last, p_side, p_inner, q_last, q_side, q_inner, biases,
     g_up, g_dn, c_up, c_dn, h_up, h_dn, a1_up, a1_dn, u1, d1, a2_up, a2_dn, u2, d2, a3_up, a3_dn,
-    x1, x1_side, row_in, corner_in, out, out_side, row_back, side_back, corner_back, tokens, padded, wqv_t, q_t, v_t, keys, att_t,
-    load_sem, store_sem, halo_send, halo_recv, back_send, back_recv,
+    x1, x1_side, row_in, corner_in, out_side, row_back, side_back, corner_back, tokens, padded, wqv_t, q_t, v_t, keys, att_t,
+    load_sem, halo_send, halo_recv, back_send, back_recv,
     core_send, core_recv, s1_send, s1_recv, s2_send, s2_recv, s3_send, s3_recv,
 ):
     lat = lax.axis_index("lat")
@@ -115,16 +116,24 @@
     def load(i, src, dst):
         return pltpu.make_async_copy(src, dst, load_sem.at[i])
 
-    loads = [
-        load(0, x2_hbm, x2),
-        load(1, cot_hbm, cot),
-        load(2, wup_hbm, wup),
-        load(3, wdown_hbm, wdown),
-        load(4, x1_hbm, x1.at[pl.ds(0, ROWS)]),
-        load(5, wqkv_hbm, wqkv),
-        load(6, wout_hbm, wout),
+    first_loads = [load(0, x2_hbm, x2), load(1, cot_hbm, cot)]
+
+    def weight_loads(j):
+        units = pl.ds(pl.multiple_of(j * CHUNK, CHUNK), CHUNK)
+        return [
+            load(2 + j, wup_hbm.at[:, units], wup.at[:, units]),
+            load(2 + CHUNKS + j, wdown_hbm.at[units], wdown.at[units]),
+        ]
+
+    later_loads = [
+        load(2 + 2 * CHUNKS + i, src, dst)
+        for i, (src, dst) in enumerate((
+            (x1_hbm, x1.at[pl.ds(0, ROWS)]), (wqkv_hbm, wqkv), (wout_hbm, wout), (bias_hbm, bias),
+            (p_last_hbm, p_last), (p_side_hbm, p_side), (p_inner_hbm, p_inner),
+            (q_last_hbm, q_last), (q_side_hbm, q_side), (q_inner_hbm, q_inner),
+        ))
     ]
-    for item in loads:
+    for item in first_loads + weight_loads(0):
         item.start()
 
     def remote(src, dst, send, recv, device):
@@ -260,8 +269,11 @@
             total += a3_dn[k].astype(F32)
         gdn_out[...] = total * (1.0 / DEVICES)
 
-    loads[0].wait()
-    loads[1].wait()
+    for item in first_loads:
+        item.wait()
+    for j in range(1, CHUNKS):
+        for item in weight_loads(j):
+            item.start()
 
     def prepare(t, carry):
         rows = pl.ds(pl.multiple_of(t * 384, 384), 384)
@@ -274,13 +286,19 @@
         return carry
 
     lax.fori_loop(0, 3, prepare, 0)
-    loads[2].wait()
-    loads[3].wait()
 
     sub = lax.broadcasted_iota(jnp.int32, (64, 8, 128), 1) < 4
 
     def chunk_step(j, carry):
         units = pl.ds(pl.multiple_of(j * CHUNK, CHUNK), CHUNK)
+        for item in weight_loads(j):
+            item.wait()
+
+        @pl.when(j == 0)
+        def _():
+            for item in later_loads:
+                item.start()
+
         w_in = wup[:, units]
         w_back = wdown[units, :]
         for t in range(2):
@@ -329,17 +347,14 @@
         mean_back = jnp.mean(back, axis=-1, keepdims=True)
         mean_both = jnp.mean(back * centred, axis=-1, keepdims=True)
         grad = cot[band].reshape(TILE, C).astype(F32) + scale * (back - mean_back - centred * mean_both)
-        x2[band] = grad.astype(BF16).reshape(WH, COLS, C)
+        gi[band] = grad.astype(BF16).reshape(WH, COLS, C)
         return carry
 
     lax.fori_loop(0, TILES, input_grad, 0)
-    store_gi = pltpu.make_async_copy(x2, gi_hbm, store_sem.at[0])
-    store_gi.start()
     core_finish(CHUNKS - 1)
 
-    loads[4].wait()
-    loads[5].wait()
-    loads[6].wait()
+    for item in later_loads:
+        item.wait()
     if comm:
         for item in halos:
             item.wait()
@@ -410,7 +425,7 @@
     tokens[0:TILE] = nn(p_last[...], cells)
     cells = jnp.concatenate(
         [x1[above, right].reshape(INNER * WH * SIDE, C), x1_side[above].reshape(INNER * WH * SIDE, C)], axis=0)
-    tokens[TILE:EDGE * WINDOW] = nn(p_side[...], cells)
+    tokens[TILE:EDGE * WINDOW] = nn(p_side[...], cells)[:INNER * WINDOW]
     project(EDGE)
     attend([1] * TILES + [0] * INNER)
     first_finish()
@@ -435,10 +450,9 @@
     for b in range(INNER):
         band = pl.ds(SHIFT_H + WH * b, WH)
         rows = slice(INNER * WINDOW * b, INNER * WINDOW * (b + 1))
-        tokens[rows] = nn(p_inner[...], x1[band].reshape(TILE, C))
+        tokens[rows] = nn(p_inner[...], x1[band].reshape(TILE, C))[:INNER * WINDOW]
     project(INNER * INNER)
     attend([0] * (INNER * INNER))
-    third_finish()
     total = feed_forward(INNER * INNER)
     for b in range(INNER):
         band = pl.ds(SHIFT_H + WH * b, WH)
@@ -447,6 +461,7 @@
         out[band, pl.ds(0, COLS - SIDE)] = cells[:, :COLS - SIDE]
         out[band, right] = out[band, right] + cells[:, COLS - SIDE:]
 
+    third_finish()
     if comm:
         for item in returns:
             item.wait()
@@ -454,10 +469,6 @@
     out[inside, left] = out[inside, left] + side_back[inside]
     out[0:SHIFT_H] = row_back[...]
     out[0:SHIFT_H, left] = out[0:SHIFT_H, left] + corner_back[...]
-    store_out = pltpu.make_async_copy(out.at[pl.ds(0, ROWS)], out_hbm, store_sem.at[1])
-    store_out.start()
-    store_gi.wait()
-    store_out.wait()
 
 
 def scratch():
@@ -470,6 +481,7 @@
         v((ROWS, COLS, C), BF16), v((ROWS, COLS, C), BF16), v((tokens, C), BF16), v((C, tokens), BF16),
         v((C, tokens), BF16), v((tokens, C), F32), v((tokens, CHUNK), BF16), v((tokens, CHUNK), BF16),
         v((C, 3 * C), BF16), v((C, C), BF16), v((C, FF), BF16), v((FF, C), BF16),
+        v((HEADS, WINDOW, WINDOW), F32), *[v(place.shape, BF16) for place in window_orders()],
         v((2, HEADS // 2, WINDOW, 256), F32),
         v((CHUNKS, 2, 64, 16, 128), BF16), v((CHUNKS, 2, 16, 16, C), BF16),
         v((CHUNKS, 64, 16, 128), BF16), v((CHUNKS, 16, 16, C), BF16),
@@ -480,14 +492,23 @@
         v((CHUNKS, 2, 2, 16, 128), BF16), v((2, 2, 16, C), BF16),
         v((3, CHUNKS, 16, 128), BF16), v((3, 16, C), BF16),
         v((ext, COLS, C), BF16), v((ext, SIDE, C), BF16), v((SHIFT_H, COLS, C), BF16),
-        v((SHIFT_H, SIDE, C), BF16), v((ext, COLS, C), BF16), v((ext, SIDE, C), BF16),
+        v((SHIFT_H, SIDE, C), BF16), v((ext, SIDE, C), BF16),
         v((SHIFT_H, COLS, C), BF16), v((ext, SIDE, C), BF16), v((SHIFT_H, SIDE, C), BF16),
         v((INNER * INNER * WINDOW, C), F32),
         v((wide, C), BF16), v((2 * C, C), BF16), v((C, wide), BF16), v((C, wide), BF16), v((wide, C), BF16), v((C, wide), BF16),
-        dma((7,)), dma((2,)), dma((3,)), dma((3,)), dma((3,)), dma((3,)),
+        dma((2 * CHUNKS + 12,)), dma((3,)), dma((3,)), dma((3,)), dma((3,)),
         dma((CHUNKS, 2)), dma((CHUNKS, 2)), dma((CHUNKS, 3, 2)), dma((CHUNKS, 3, 2)),
         dma((3, 2)), dma((3, 2)), dma((3, 2)), dma((3, 2)),
     ]
+
+
+def place_results(first, grad, up, down, first_out, grad_out, up_out, down_out, sem):
+    pairs = [(first.at[pl.ds(0, ROWS)], first_out), (grad, grad_out), (up, up_out), (down, down_out)]
+    copies = [pltpu.make_async_copy(src, dst, sem.at[i]) for i, (src, dst) in enumerate(pairs)]
+    for copy in copies:
+        copy.start()
+    for copy in copies:
+        copy.wait()
 
 
 def shards(comm, x_first, x_second, cotangent, gain_attn, gain_mlp, w_qkv, w_out, w_up, w_down, bias):
@@ -497,26 +518,39 @@
     params = dict(vmem_limit_bytes=60 * 1024 * 1024, has_side_effects=True)
     if comm:
         params["collective_id"] = 0
-    out_first, grad_input, up, down = pl.pallas_call(
+    results = pl.pallas_call(
         functools.partial(kernel, comm),
+        out_shape=(
+            pltpu.VMEM((ROWS + SHIFT_H, COLS, C), BF16),
+            pltpu.VMEM((ROWS, COLS, C), BF16),
+            pltpu.VMEM((4, FF), F32),
+            pltpu.VMEM((16, C), F32),
+        ),
+        in_specs=[anywhere] * 14 + [near] * 2,
+        out_specs=(near,) * 4,
+        scratch_shapes=scratch(),
+        compiler_params=pltpu.CompilerParams(**params),
+        cost_estimate=pl.CostEstimate(flops=20 * 10**9, bytes_accessed=13 * 10**6, transcendentals=10**7),
+        name="swin_block",
+    )(
+        x_first, x_second, cotangent, w_qkv, w_out, w_up, w_down,
+        bias, *[jnp.asarray(place, BF16) for place in places],
+        gain_attn.reshape(1, C), gain_mlp.reshape(1, C),
+    )
+    return pl.pallas_call(
+        place_results,
         out_shape=(
             jax.ShapeDtypeStruct((ROWS, COLS, C), BF16),
             jax.ShapeDtypeStruct((ROWS, COLS, C), BF16),
             jax.ShapeDtypeStruct((4, FF), F32),
             jax.ShapeDtypeStruct((16, C), F32),
         ),
-        in_specs=[anywhere] * 7 + [near] * 9,
-        out_specs=(anywhere, anywhere, near, near),
-        scratch_shapes=scratch(),
-        compiler_params=pltpu.CompilerParams(**params),
-        cost_estimate=pl.CostEstimate(flops=20 * 10**9, bytes_accessed=13 * 10**6, transcendentals=10**7),
-        name="swin_block",
-    )(
-        x_first, x_second, cotangent, w_qkv, w_out, w_up, w_down,
-        gain_attn.reshape(1, C), gain_mlp.reshape(1, C), bias,
-        *[jnp.asarray(place, BF16) for place in places], *[jnp.asarray(place.T, BF16) for place in places],
-    )
-    return out_first, grad_input, up, down
+        in_specs=[near] * 4,
+        out_specs=(anywhere,) * 4,
+        scratch_shapes=[pltpu.SemaphoreType.DMA((4,))],
+        compiler_params=pltpu.CompilerParams(vmem_limit_bytes=1024 * 1024),
+        name="place_results",
+    )(*[pltpu.with_memory_space_constraint(item, pltpu.VMEM) for item in results])
 
 
 def solution(mesh):

time: 57.8 us -> 50.8 us (0.88)
  local copies, waits for them, and re-layouts: 4.71 us -> 0 us
  Pallas kernels: 52.3 us -> 49.5 us
    unnamed x10 -> x0, local copies, waits for them, and re-layouts: 4.71 us -> none
    pallas_call x1 -> x2, Pallas kernels: 52.3 us -> 49.5 us  [the longest x1 48 us: shards(): pl.pallas_call(functools.partial(kernel, comm), out_shape=(pltpu.VMEM((RO...]
where the time goes in v3:
time: 50.8 us; the launch traced here: 50.3 us
  Pallas kernels  49.5 us (97%)
  between operations  0.8 us (2%)
    pallas_call x1, Pallas kernels, shards(): pl.pallas_call(functools.partial(kernel, comm), out_shape=(pltpu.VMEM((RO...  48 us
    pallas_call x1, Pallas kernels, shards(): pl.pallas_call(place_results, out_shape=(jax.ShapeDtypeStruct((ROWS, COLS...  1.44 us

profile of v3, /device:TPU:1, one launch (start us, length us, event | category | flops | bytes accessed | tf_op | source)
XLA Modules:
  0.0 50.3 jit_solution(881009054536939552)
XLA Ops:
  0.6 48.0 %swin_block.1 = (bf16[27,48,512]{2,1,0:T(8,128)(2,1)S(1)}, bf16[24,48,512]{2,1,0:T(8,128)(2,1)S(1)}, f32[4,2048]{1,0:T(4,128)S(1)}, f32[16,512]{1,0:T(8,128)S(1)}) custom-call(bf16[24,48,512]{2,1,0:T(8,128)(2,1)} %x1_hbm.1, bf16[24,48,512]{2,1,0:T(8,128)(2,1)} %x2_hbm.1, bf16[24,48,512]{2,1,0:T(8,128)(2,1)} %cot_hbm.1, bf16[512,1536]{1,0:T(8,128)(2,1)} %wqkv_hbm.1, ...), custom_call_target="tpu_custom_call" | custom-call | flops 20000000000 | bytes 13000000 | tf_op jit(solution)/shard_map/swin_block/pallas_call | solution.py:521
  48.7 1.4 %place_results.1 = (bf16[24,48,512]{2,1,0:T(8,128)(2,1)}, bf16[24,48,512]{2,1,0:T(8,128)(2,1)}, f32[4,2048]{1,0:T(4,128)}, f32[16,512]{1,0:T(8,128)}) custom-call(bf16[27,48,512]{2,1,0:T(8,128)(2,1)S(1)} %get-tuple-element.8.first, bf16[24,48,512]{2,1,0:T(8,128)(2,1)S(1)} %get-tuple-element.9.grad, f32[4,2048]{1,0:T(4,128)S(1)} %get-tuple-element.10.up, ...), custom_call_target="tpu_custom_call" | custom-call | tf_op jit(solution)/shard_map/place_results/pallas_call | solution.py:540

commit v4 on v3

--- a/solution.py
+++ b/solution.py
@@ -128,12 +128,13 @@
     later_loads = [
         load(2 + 2 * CHUNKS + i, src, dst)
         for i, (src, dst) in enumerate((
-            (x1_hbm, x1.at[pl.ds(0, ROWS)]), (wqkv_hbm, wqkv), (wout_hbm, wout), (bias_hbm, bias),
+            (x1_hbm, x1.at[pl.ds(0, ROWS)]), (wqkv_hbm, wqkv), (wout_hbm, wout),
             (p_last_hbm, p_last), (p_side_hbm, p_side), (p_inner_hbm, p_inner),
             (q_last_hbm, q_last), (q_side_hbm, q_side), (q_inner_hbm, q_inner),
         ))
     ]
-    for item in first_loads + weight_loads(0):
+    bias_load = load(11 + 2 * CHUNKS, bias_hbm, bias)
+    for item in [bias_load] + first_loads + weight_loads(0):
         item.start()
 
     def remote(src, dst, send, recv, device):
@@ -268,6 +269,18 @@
         for k in range(3):
             total += a3_dn[k].astype(F32)
         gdn_out[...] = total * (1.0 / DEVICES)
+
+    bias_load.wait()
+    upper_q = lax.broadcasted_iota(jnp.int32, (WINDOW, WINDOW), 0) < WINDOW // 2
+    upper_k = lax.broadcasted_iota(jnp.int32, (WINDOW, WINDOW), 1) < WINDOW // 2
+    split = jnp.where(upper_q == upper_k, 0.0, jnp.where(lat == 7, FAR, 0.0))
+    biases[...] = jnp.zeros(biases.shape, F32)
+    for head in range(HEADS):
+        lanes = pl.ds(128 * (head % 2), WINDOW)
+        turned = bias[head].T
+        biases[0, head // 2, :, lanes] = turned
+        biases[1, head // 2, :, lanes] = turned + split
+    padded[...] = jnp.zeros(padded.shape, BF16)
 
     for item in first_loads:
         item.wait()
@@ -360,16 +373,6 @@
             item.wait()
     x1[ROWS:ROWS + SHIFT_H] = row_in[...]
     x1_side[ROWS:ROWS + SHIFT_H] = corner_in[...]
-    upper_q = lax.broadcasted_iota(jnp.int32, (WINDOW, WINDOW), 0) < WINDOW // 2
-    upper_k = lax.broadcasted_iota(jnp.int32, (WINDOW, WINDOW), 1) < WINDOW // 2
-    split = jnp.where(upper_q == upper_k, 0.0, jnp.where(lat == 7, FAR, 0.0))
-    biases[...] = jnp.zeros(biases.shape, F32)
-    for head in range(HEADS):
-        lanes = pl.ds(128 * (head % 2), WINDOW)
-        turned = bias[head].T
-        biases[0, head // 2, :, lanes] = turned
-        biases[1, head // 2, :, lanes] = turned + split
-    padded[...] = jnp.zeros(padded.shape, BF16)
     wqv_t[0:C] = wqkv[:, 0:C].T
     wqv_t[C:2 * C] = wqkv[:, 2 * C:3 * C].T
     upper = lax.broadcasted_iota(jnp.int32, (128, 128), 0) < 64
@@ -389,15 +392,18 @@
     def attend(masks):
         def pair_step(pair, carry):
             heads = pl.ds(pl.multiple_of(pair * 128, 128), 128)
+            scores, weights = [], []
             for w, masked in enumerate(masks):
-                cells = slice(w * 128, (w + 1) * 128)
-                query = q_t[heads, cells]
+                query = q_t[heads, w * 128:(w + 1) * 128]
                 query = jnp.concatenate(
                     [jnp.where(upper, query, nothing), jnp.where(upper, nothing, query)], axis=1)
-                scores = nn(keys[w * 128:w * 128 + WINDOW, heads], query) + biases[masked, pair]
-                raised = jnp.exp(scores - jnp.max(scores, axis=0, keepdims=True))
-                inverse = 1.0 / jnp.sum(raised, axis=0, keepdims=True)
-                blended = nn(v_t[heads, cells], jnp.concatenate([raised.astype(BF16), gap], axis=0)) * inverse
+                scores.append(nn(keys[w * 128:w * 128 + WINDOW, heads], query) + biases[masked, pair])
+            for score in scores:
+                raised = jnp.exp(score - jnp.max(score, axis=0, keepdims=True))
+                weights.append((raised.astype(BF16), 1.0 / jnp.sum(raised, axis=0, keepdims=True)))
+            for w, (raised, inverse) in enumerate(weights):
+                cells = slice(w * 128, (w + 1) * 128)
+                blended = nn(v_t[heads, cells], jnp.concatenate([raised, gap], axis=0)) * inverse
                 att_t[heads, cells] = jnp.where(upper, blended[:, :128], blended[:, 128:]).astype(BF16)
             return carry
 
@@ -411,10 +417,13 @@
         mid, _ = normalize(residual)
         mid = (mid * gain_mlp[...]).astype(BF16)
         total = residual
+        units = [slice(j * CHUNK, (j + 1) * CHUNK) for j in range(CHUNKS)]
+        ready = nn(mid, wup[:, units[0]])
         for j in range(CHUNKS):
-            units = slice(j * CHUNK, (j + 1) * CHUNK)
-            hidden = gelu(nn(mid, wup[:, units])).astype(BF16)
-            total = total + nn(hidden, wdown[units, :])
+            coming = nn(mid, wup[:, units[j + 1]]) if j + 1 < CHUNKS else None
+            hidden = gelu(ready).astype(BF16)
+            total = total + nn(hidden, wdown[units[j], :])
+            ready = coming
         return total
 
     above = pl.ds(SHIFT_H, INNER * WH)
@@ -445,13 +454,13 @@
     if comm:
         for item in returns:
             item.start()
-    second_finish()
 
     for b in range(INNER):
         band = pl.ds(SHIFT_H + WH * b, WH)
         rows = slice(INNER * WINDOW * b, INNER * WINDOW * (b + 1))
         tokens[rows] = nn(p_inner[...], x1[band].reshape(TILE, C))[:INNER * WINDOW]
     project(INNER * INNER)
+    second_finish()
     attend([0] * (INNER * INNER))
     total = feed_forward(INNER * INNER)
     for b in range(INNER):

time: 50.8 us -> 49.3 us (0.970)
  Pallas kernels: 49.5 us -> 48.3 us
    pallas_call x1, Pallas kernels: 48 us -> 46.9 us  [shards(): pl.pallas_call(functools.partial(kernel, comm), out_shape=(pltpu.VMEM((RO...]
where the time goes in v4:
time: 49.3 us; the launch traced here: 49.1 us
  Pallas kernels  48.3 us (98%)
  between operations  0.8 us (2%)
    pallas_call x1, Pallas kernels, shards(): pl.pallas_call(functools.partial(kernel, comm), out_shape=(pltpu.VMEM((RO...  46.9 us
    pallas_call x1, Pallas kernels, shards(): pl.pallas_call(place_results, out_shape=(jax.ShapeDtypeStruct((ROWS, COLS...  1.44 us

profile of v4, /device:TPU:1, one launch (start us, length us, event | category | flops | bytes accessed | tf_op | source)
XLA Modules:
  0.0 49.1 jit_solution(14417589366636427250)
XLA Ops:
  0.6 46.9 %swin_block.1 = (bf16[27,48,512]{2,1,0:T(8,128)(2,1)S(1)}, bf16[24,48,512]{2,1,0:T(8,128)(2,1)S(1)}, f32[4,2048]{1,0:T(4,128)S(1)}, f32[16,512]{1,0:T(8,128)S(1)}) custom-call(bf16[24,48,512]{2,1,0:T(8,128)(2,1)} %x1_hbm.1, bf16[24,48,512]{2,1,0:T(8,128)(2,1)} %x2_hbm.1, bf16[24,48,512]{2,1,0:T(8,128)(2,1)} %cot_hbm.1, bf16[512,1536]{1,0:T(8,128)(2,1)} %wqkv_hbm.1, ...), custom_call_target="tpu_custom_call" | custom-call | flops 20000000000 | bytes 13000000 | tf_op jit(solution)/shard_map/swin_block/pallas_call | solution.py:530
  47.5 1.4 %place_results.1 = (bf16[24,48,512]{2,1,0:T(8,128)(2,1)}, bf16[24,48,512]{2,1,0:T(8,128)(2,1)}, f32[4,2048]{1,0:T(4,128)}, f32[16,512]{1,0:T(8,128)}) custom-call(bf16[27,48,512]{2,1,0:T(8,128)(2,1)S(1)} %get-tuple-element.8.first, bf16[24,48,512]{2,1,0:T(8,128)(2,1)S(1)} %get-tuple-element.9.grad, f32[4,2048]{1,0:T(4,128)S(1)} %get-tuple-element.10.up, ...), custom_call_target="tpu_custom_call" | custom-call | tf_op jit(solution)/shard_map/place_results/pallas_call | solution.py:549

commit v5 on v4

--- a/solution.py
+++ b/solution.py
@@ -160,14 +160,14 @@
             (lat_next, lon), (lat_prev, lon), (lat, lon_next), (lat, lon_prev),
             (lat_next, lon_next), (lat_prev, lon_prev), core_peer(),
         ]
-        for k in (1, 2, 3):
+        for k in (2, 1, 3):
             peers += [x_peer(k)[1], z_peer(k)[1], y_peer(k)[2]]
         for peer in peers:
             pl.semaphore_signal(barrier, inc=1, device_id=peer, device_id_type=MESH)
 
     def meet():
         pl.semaphore_wait(barrier, len(peers))
-        for item in halos:
+        for item in (halos[1], halos[0], halos[2]):
             item.start()
 
     def core_copies(j):
@@ -179,7 +179,7 @@
 
     def first_copies(j):
         copies = []
-        for k in (1, 2, 3):
+        for k in (2, 1, 3):
             other, device = z_peer(k)
             copies.append(remote(
                 h_up.at[j, :, other], a1_up.at[k - 1, j], s1_send.at[j, k - 1, 0], s1_recv.at[j, k - 1, 0], device))
@@ -190,7 +190,7 @@
 
     def second_copies():
         copies = []
-        for k in (1, 2, 3):
+        for k in (2, 1, 3):
             other, device = x_peer(k)
             copies.append(remote(
                 u1.at[:, :, other], a2_up.at[k - 1], s2_send.at[k - 1, 0], s2_recv.at[k - 1, 0], device))
@@ -201,7 +201,7 @@
 
     def third_copies():
         copies = []
-        for k in (1, 2, 3):
+        for k in (2, 1, 3):
             lo, hi, device = y_peer(k)
             copies.append(remote(
                 u2.at[:, lo, hi], a3_up.at[k - 1], s3_send.at[k - 1, 0], s3_recv.at[k - 1, 0], device))
@@ -452,7 +452,7 @@
         remote(out_side.at[tail], corner_back, back_send.at[2], back_recv.at[2], (lat_next, lon_next)),
     ]
     if comm:
-        for item in returns:
+        for item in (returns[1], returns[0], returns[2]):
             item.start()
 
     for b in range(INNER):

time: 49.3 us -> 50.4 us (1.022)
  Pallas kernels: 48.3 us -> 49.5 us
    pallas_call x1, Pallas kernels: 46.9 us -> 48 us  [shards(): pl.pallas_call(functools.partial(kernel, comm), out_shape=(pltpu.VMEM((RO...]
where the time goes in v5:
time: 50.4 us; the launch traced here: 50.3 us
  Pallas kernels  49.5 us (98%)
  between operations  0.8 us (2%)
    pallas_call x1, Pallas kernels, shards(): pl.pallas_call(functools.partial(kernel, comm), out_shape=(pltpu.VMEM((RO...  48 us
    pallas_call x1, Pallas kernels, shards(): pl.pallas_call(place_results, out_shape=(jax.ShapeDtypeStruct((ROWS, COLS...  1.44 us

profile of v5, /device:TPU:1, one launch (start us, length us, event | category | flops | bytes accessed | tf_op | source)
XLA Modules:
  0.0 50.3 jit_solution(14318390948939725042)
XLA Ops:
  0.6 48.0 %swin_block.1 = (bf16[27,48,512]{2,1,0:T(8,128)(2,1)S(1)}, bf16[24,48,512]{2,1,0:T(8,128)(2,1)S(1)}, f32[4,2048]{1,0:T(4,128)S(1)}, f32[16,512]{1,0:T(8,128)S(1)}) custom-call(bf16[24,48,512]{2,1,0:T(8,128)(2,1)} %x1_hbm.1, bf16[24,48,512]{2,1,0:T(8,128)(2,1)} %x2_hbm.1, bf16[24,48,512]{2,1,0:T(8,128)(2,1)} %cot_hbm.1, bf16[512,1536]{1,0:T(8,128)(2,1)} %wqkv_hbm.1, ...), custom_call_target="tpu_custom_call" | custom-call | flops 20000000000 | bytes 13000000 | tf_op jit(solution)/shard_map/swin_block/pallas_call | solution.py:530
  48.7 1.4 %place_results.1 = (bf16[24,48,512]{2,1,0:T(8,128)(2,1)}, bf16[24,48,512]{2,1,0:T(8,128)(2,1)}, f32[4,2048]{1,0:T(4,128)}, f32[16,512]{1,0:T(8,128)}) custom-call(bf16[27,48,512]{2,1,0:T(8,128)(2,1)S(1)} %get-tuple-element.8.first, bf16[24,48,512]{2,1,0:T(8,128)(2,1)S(1)} %get-tuple-element.9.grad, f32[4,2048]{1,0:T(4,128)S(1)} %get-tuple-element.10.up, ...), custom_call_target="tpu_custom_call" | custom-call | tf_op jit(solution)/shard_map/place_results/pallas_call | solution.py:549
